TPU v7x, 32 devices: a whole 2x2x4 slice. The times are simulated.
32 devices in a mesh: layer: 4 (over y, core), tx: 2 (over x), ty: 4 (over z).
Axes of the slice: x: 2, y: 2, z: 4, core: 2. Of those that a mesh axis runs over, the one named last changes fastest.
Arguments:
- layers: float32 [4, 256, 2048], P('layer', 'tx', 'ty'), may hold values from -6 to 6
- wind: int32 [4, 2], P('layer'), may hold values from -128 to 128
- offsets: int32 [4, 9, 2], P('layer'), may hold values from -64 to 64
- weights: bfloat16 [9, 2, 256, 2048], P(None, None, 'tx', 'ty'), may hold values from -0.5 to 0.5
- sub_index: int32 [256, 2048], P('tx', 'ty'), may hold values from -1 to 255, as said below
Outputs:
- slopes: float32 [2, 9, 32, 256], P(None, None, 'tx', 'ty')
Inputs may be any that keep to these rules, and one draw needn't show every extreme that they name: sub_index[i, j] is -1 or j // 8.
All inputs are finite; a program needn't handle non-finite values.
Results may differ from a plain program's by a relative error of at most 0.0003.
Values sent between devices are 32-bit elements; how exact they have to be, the bound alone decides.
A program may use at most 256 MiB of HBM per device.

v0:
```python
import jax
import jax.numpy as jnp
from jax import lax
from jax.sharding import PartitionSpec as P

DIRS = 9
SUB = 8
HMAX = 2
FOOT = 64


def padded(cells, sides, width):
    for axis, dim in sides:
        count = lax.axis_size(axis)
        head = lax.slice_in_dim(cells, 0, width, axis=dim)
        tail = lax.slice_in_dim(cells, cells.shape[dim] - width, cells.shape[dim], axis=dim)
        cells = jnp.concatenate(
            [
                lax.ppermute(tail, axis, [(i, (i + 1) % count) for i in range(count)]),
                cells,
                lax.ppermute(head, axis, [((i + 1) % count, i) for i in range(count)]),
            ],
            axis=dim,
        )
    return cells


def shift_stack(extended, quotient, fraction, out_rows, out_cols):
    margin = HMAX + 1
    field = extended[0]
    start_row = margin - quotient[0, 0]
    start_col = margin - quotient[0, 1]
    corner_aa = lax.dynamic_slice(field, (start_row, start_col), (out_rows, out_cols))
    corner_ab = lax.dynamic_slice(field, (start_row, start_col - 1), (out_rows, out_cols))
    corner_ba = lax.dynamic_slice(field, (start_row - 1, start_col), (out_rows, out_cols))
    corner_bb = lax.dynamic_slice(field, (start_row - 1, start_col - 1), (out_rows, out_cols))
    frow = fraction[0, 0]
    fcol = fraction[0, 1]
    pieces = [
        (1.0 - frow) * ((1.0 - fcol) * corner_aa + fcol * corner_ab)
        + frow * ((1.0 - fcol) * corner_ba + fcol * corner_bb)
    ]
    return jnp.stack(pieces)


def on_device(layers, wind, offsets, weights, sub_index):
    count, rows, cols = layers.shape
    quotient = jnp.floor_divide(wind, 64)
    fraction = (wind - 64 * quotient).astype(jnp.float32) / 64.0
    rimmed = padded(layers, (("tx", 1), ("ty", 2)), HMAX + 1)
    shifted = shift_stack(rimmed, quotient, fraction, rows, cols)
    spread = padded(shifted, (("tx", 1), ("ty", 2)), FOOT)
    live = (sub_index >= 0).astype(jnp.float32)
    results = []
    for d in range(DIRS):
        start_row = FOOT + offsets[0, d, 0]
        start_col = FOOT + offsets[0, d, 1]
        total = lax.dynamic_slice(spread[0], (start_row, start_col), (rows, cols))
        masked = total * live
        terms = weights[d].astype(jnp.float32) * masked[None]
        results.append(terms.reshape(2, rows // SUB, SUB, cols // SUB, SUB).sum(axis=(2, 4)))
    local_slopes = jnp.stack(results, axis=1)
    return lax.psum(local_slopes, "layer")


def solution(mesh):
    placed = (
        P("layer", "tx", "ty"),
        P("layer", None),
        P("layer", None, None),
        P(None, None, "tx", "ty"),
        P("tx", "ty"),
    )
    return jax.shard_map(
        on_device, mesh=mesh, in_specs=placed, out_specs=P(None, None, "tx", "ty"), check_vma=False
    )
```

profile of v0, /device:TPU:0, one launch (start us, length us, event | category | flops | bytes accessed | tf_op | source)
XLA Modules:
  0.0 238.4 jit_solution(12341837292214623267)
XLA Ops:
  7.3 2.9 %collective-permute-start.1 = (f32[1,3,512]{2,1,0:T(4,128)S(1)}, f32[1,3,512]{2,1,0:T(4,128)S(1)}, u32[]{:S(2)}, u32[]{:S(2)}) collective-permute-start(f32[1,3,512]{2,1,0:T(4,128)S(1)} %get-tuple-element.33), channel_id=1, source_target_pairs={{4,0},{0,4},{5,1},{1,5},{6,2},{2,6},{7,3},{3,7},{12,8},{8,12},{13,... | collective-permute-start | bytes 18440 | tf_op jit(solution)/shard_map/ppermute | solution.py:21
  15.6 4.1 %collective-permute-start.3 = (f32[1,134,3]{2,1,0:T(8,128)S(1)}, f32[1,134,3]{2,1,0:T(8,128)S(1)}, u32[]{:S(2)}, u32[]{:S(2)}) collective-permute-start(f32[1,134,3]{2,1,0:T(8,128)S(1)} %get-tuple-element.29), channel_id=1, source_target_pairs={{1,0},{2,1},{3,2},{0,3},{5,4},{6,5},{7,6},{4,7},{9,8},{10,9},{11,1... | collective-permute-start | bytes 4832 | tf_op jit(solution)/shard_map/ppermute | solution.py:21
  23.4 2.4 %collective-permute-done.2 = f32[1,134,3]{2,1,0:T(8,128)S(1)} collective-permute-done((f32[1,134,3]{2,1,0:T(8,128)S(1)}, f32[1,134,3]{2,1,0:T(8,128)S(1)}, u32[]{:S(2)}, u32[]{:S(2)}) %collective-permute-start.2) | collective-permute-done | bytes 1640 | tf_op jit(solution)/shard_map/ppermute | solution.py:19
  30.7 3.2 %slice_convert_fusion = (f32[1,2,128,512]{3,2,1,0:T(8,128)S(1)}, f32[1,2,128,512]{3,2,1,0:T(8,128)S(1)}, f32[1,2,128,512]{3,2,1,0:T(8,128)S(1)}, f32[1,2,128,512...) fusion(bf16[9,2,128,512]{3,2,1,0:T(8,128)(2,1)} %param.8), kind=kLoop, calls=%fused_computation.20 | loop fusion | flops 1179648 | bytes 7077888 | tf_op jit(solution)/shard_map/convert_element_type | solution.py:60
  61.0 7.1 %reshape.200 = f32[2,16,8,64,8]{4,3,2,1,0:T(8,128)} reshape(f32[1,2,128,512]{3,2,1,0:T(8,128)} %get-tuple-element.16) | data formatting | bytes 1048576 | tf_op jit(solution)/shard_map/convert_element_type | solution.py:60
  68.1 7.0 %reshape.201 = f32[2,16,8,64,8]{4,3,2,1,0:T(8,128)} reshape(f32[1,2,128,512]{3,2,1,0:T(8,128)} %get-tuple-element.15) | data formatting | bytes 1048576 | tf_op jit(solution)/shard_map/convert_element_type | solution.py:60
  75.1 7.1 %reshape.202 = f32[2,16,8,64,8]{4,3,2,1,0:T(8,128)} reshape(f32[1,2,128,512]{3,2,1,0:T(8,128)} %get-tuple-element.14) | data formatting | bytes 1048576 | tf_op jit(solution)/shard_map/convert_element_type | solution.py:60
  82.2 6.1 %reshape.203 = f32[2,16,8,64,8]{4,3,2,1,0:T(8,128)} reshape(f32[1,2,128,512]{3,2,1,0:T(8,128)S(1)} %get-tuple-element.13) | data formatting | bytes 1048576 | tf_op jit(solution)/shard_map/convert_element_type | solution.py:60
  88.3 6.2 %reshape.204 = f32[2,16,8,64,8]{4,3,2,1,0:T(8,128)} reshape(f32[1,2,128,512]{3,2,1,0:T(8,128)S(1)} %get-tuple-element.12) | data formatting | bytes 1048576 | tf_op jit(solution)/shard_map/convert_element_type | solution.py:60
  94.5 6.1 %reshape.205 = f32[2,16,8,64,8]{4,3,2,1,0:T(8,128)} reshape(f32[1,2,128,512]{3,2,1,0:T(8,128)S(1)} %get-tuple-element.11) | data formatting | bytes 1048576 | tf_op jit(solution)/shard_map/convert_element_type | solution.py:60
  100.6 6.1 %reshape.206 = f32[2,16,8,64,8]{4,3,2,1,0:T(8,128)} reshape(f32[1,2,128,512]{3,2,1,0:T(8,128)S(1)} %get-tuple-element.10) | data formatting | bytes 1048576 | tf_op jit(solution)/shard_map/convert_element_type | solution.py:60
  106.7 6.1 %reshape.207 = f32[2,16,8,64,8]{4,3,2,1,0:T(8,128)} reshape(f32[1,2,128,512]{3,2,1,0:T(8,128)S(1)} %get-tuple-element.17) | data formatting | bytes 1048576 | tf_op jit(solution)/shard_map/convert_element_type | solution.py:60
  112.8 6.1 %reshape.208 = f32[2,16,8,64,8]{4,3,2,1,0:T(8,128)} reshape(f32[1,2,128,512]{3,2,1,0:T(8,128)S(1)} %get-tuple-element.9) | data formatting | bytes 1048576 | tf_op jit(solution)/shard_map/convert_element_type | solution.py:60
  121.1 3.7 %mul.215 = f32[16,8,64,8]{3,2,1,0:T(8,128)} reshape(f32[128,512]{1,0:T(8,128)S(1)} %get-tuple-element.25) | data formatting | bytes 524288 | tf_op jit(solution)/shard_map/mul | solution.py:60
  124.8 5.9 %multiply_reduce_fusion.8 = f32[2,16,64]{2,1,0:T(8,128)S(1)} fusion(f32[2,16,8,64,8]{4,3,2,1,0:T(8,128)} %reshape.200, f32[16,8,64,8]{3,2,1,0:T(8,128)} %mul.215), kind=kLoop, calls=%fused_computation.8 | loop fusion | flops 260096 | bytes 794624 | tf_op jit(solution)/shard_map/reduce_sum | solution.py:61
  130.7 3.7 %mul.219 = f32[16,8,64,8]{3,2,1,0:T(8,128)} reshape(f32[128,512]{1,0:T(8,128)S(1)} %get-tuple-element.24) | data formatting | bytes 524288 | tf_op jit(solution)/shard_map/mul | solution.py:60
  134.3 3.6 %mul.223 = f32[16,8,64,8]{3,2,1,0:T(8,128)} reshape(f32[128,512]{1,0:T(8,128)S(1)} %get-tuple-element.23) | data formatting | bytes 524288 | tf_op jit(solution)/shard_map/mul | solution.py:60
  137.9 3.6 %mul.227 = f32[16,8,64,8]{3,2,1,0:T(8,128)} reshape(f32[128,512]{1,0:T(8,128)S(1)} %get-tuple-element.22) | data formatting | bytes 524288 | tf_op jit(solution)/shard_map/mul | solution.py:60
  141.6 3.7 %mul.231 = f32[16,8,64,8]{3,2,1,0:T(8,128)} reshape(f32[128,512]{1,0:T(8,128)S(1)} %get-tuple-element.21) | data formatting | bytes 524288 | tf_op jit(solution)/shard_map/mul | solution.py:60
  145.2 3.6 %mul.235 = f32[16,8,64,8]{3,2,1,0:T(8,128)} reshape(f32[128,512]{1,0:T(8,128)S(1)} %get-tuple-element.20) | data formatting | bytes 524288 | tf_op jit(solution)/shard_map/mul | solution.py:60
  148.8 3.7 %mul.239 = f32[16,8,64,8]{3,2,1,0:T(8,128)} reshape(f32[128,512]{1,0:T(8,128)S(1)} %get-tuple-element.19) | data formatting | bytes 524288 | tf_op jit(solution)/shard_map/mul | solution.py:60
  152.5 3.6 %mul.243 = f32[16,8,64,8]{3,2,1,0:T(8,128)} reshape(f32[128,512]{1,0:T(8,128)S(1)} %get-tuple-element.18) | data formatting | bytes 524288 | tf_op jit(solution)/shard_map/mul | solution.py:60
  156.1 3.7 %mul.247 = f32[16,8,64,8]{3,2,1,0:T(8,128)} reshape(f32[128,512]{1,0:T(8,128)S(1)} %get-tuple-element.5) | data formatting | bytes 524288 | tf_op jit(solution)/shard_map/mul | solution.py:60
  159.8 6.0 %multiply_reduce_fusion.7 = f32[2,16,64]{2,1,0:T(8,128)S(1)} fusion(f32[2,16,8,64,8]{4,3,2,1,0:T(8,128)} %reshape.201, f32[16,8,64,8]{3,2,1,0:T(8,128)} %mul.219), kind=kLoop, calls=%fused_computation.7 | loop fusion | flops 260096 | bytes 794624 | tf_op jit(solution)/shard_map/reduce_sum | solution.py:61
  165.9 5.0 %multiply_reduce_fusion.6 = f32[2,16,64]{2,1,0:T(8,128)S(1)} fusion(f32[2,16,8,64,8]{4,3,2,1,0:T(8,128)} %reshape.202, f32[16,8,64,8]{3,2,1,0:T(8,128)S(1)} %copy-done.1), kind=kLoop, calls=%fused_computation.6 | loop fusion | flops 260096 | bytes 794624 | tf_op jit(solution)/shard_map/reduce_sum | solution.py:61
  170.9 5.0 %multiply_reduce_fusion.5 = f32[2,16,64]{2,1,0:T(8,128)S(1)} fusion(f32[2,16,8,64,8]{4,3,2,1,0:T(8,128)} %reshape.203, f32[16,8,64,8]{3,2,1,0:T(8,128)S(1)} %copy-done), kind=kLoop, calls=%fused_computation.5 | loop fusion | flops 260096 | bytes 794624 | tf_op jit(solution)/shard_map/reduce_sum | solution.py:61
  176.0 3.8 %multiply_reduce_fusion.4 = f32[2,16,64]{2,1,0:T(8,128)S(1)} fusion(f32[2,16,8,64,8]{4,3,2,1,0:T(8,128)S(1)} %bitcast.107, f32[16,8,64,8]{3,2,1,0:T(8,128)} %mul.231), kind=kLoop, calls=%fused_computation.4 | loop fusion | flops 260096 | bytes 794624 | tf_op jit(solution)/shard_map/reduce_sum | solution.py:61
  179.8 3.8 %multiply_reduce_fusion.3 = f32[2,16,64]{2,1,0:T(8,128)S(1)} fusion(f32[2,16,8,64,8]{4,3,2,1,0:T(8,128)S(1)} %bitcast.105, f32[16,8,64,8]{3,2,1,0:T(8,128)} %mul.235), kind=kLoop, calls=%fused_computation.3 | loop fusion | flops 260096 | bytes 794624 | tf_op jit(solution)/shard_map/reduce_sum | solution.py:61
  183.6 6.0 %multiply_reduce_fusion.2 = f32[2,16,64]{2,1,0:T(8,128)S(1)} fusion(f32[2,16,8,64,8]{4,3,2,1,0:T(8,128)} %reshape.206, f32[16,8,64,8]{3,2,1,0:T(8,128)} %mul.239), kind=kLoop, calls=%fused_computation.2 | loop fusion | flops 260096 | bytes 794624 | tf_op jit(solution)/shard_map/reduce_sum | solution.py:61
  189.6 3.8 %multiply_reduce_fusion.1 = f32[2,16,64]{2,1,0:T(8,128)S(1)} fusion(f32[2,16,8,64,8]{4,3,2,1,0:T(8,128)S(1)} %bitcast.103, f32[16,8,64,8]{3,2,1,0:T(8,128)} %mul.243), kind=kLoop, calls=%fused_computation.1 | loop fusion | flops 260096 | bytes 794624 | tf_op jit(solution)/shard_map/reduce_sum | solution.py:61
  193.4 3.6 %multiply_reduce_fusion = f32[2,16,64]{2,1,0:T(8,128)S(1)} fusion(f32[2,16,8,64,8]{4,3,2,1,0:T(8,128)S(1)} %bitcast.101, f32[16,8,64,8]{3,2,1,0:T(8,128)} %mul.247), kind=kLoop, calls=%fused_computation | loop fusion | flops 260096 | bytes 794624 | tf_op jit(solution)/shard_map/reduce_sum | solution.py:61
  197.8 32.3 %all-reduce.2.cloned.1.call-done = f32[2,9,16,64]{3,2,1,0:T(8,128)} async-done(((f32[2,9,16,64]{3,2,1,0:T(8,128)}), f32[2,9,16,64]{3,2,1,0:T(8,128)}) %all-reduce.2.cloned.1.call-update) | async-done | bytes 73744 | tf_op jit(solution)/shard_map/psum | solution.py:63
  (72 shorter events, 18.3 us)
Async XLA Ops:
  6.5 32.0 %copy-start.6 = (s32[1,9,2]{1,2,0:T(2,128)S(1)}, s32[1,9,2]{1,2,0:T(2,128)}, u32[]{:S(2)}) copy-start(s32[1,9,2]{1,2,0:T(2,128)} %param.7) | copy-start | bytes 220
  6.5 223.5 %all-reduce.2.cloned.1.call-start = ((), (), s32[]{:S(2)}) async-start(), calls=%async_computation | async-start | bytes 294912 | tf_op jit(solution)/shard_map/psum | solution.py:63
  7.3 7.3 %collective-permute-start.1 = (f32[1,3,512]{2,1,0:T(4,128)S(1)}, f32[1,3,512]{2,1,0:T(4,128)S(1)}, u32[]{:S(2)}, u32[]{:S(2)}) collective-permute-start(f32[1,3,512]{2,1,0:T(4,128)S(1)} %get-tuple-element.33), channel_id=1, source_target_pairs={{4,0},{0,4},{5,1},{1,5},{6,2},{2,6},{7,3},{3,7},{12,8},{8,12},{13,... | collective-permute-start | bytes 18440 | tf_op jit(solution)/shard_map/ppermute | solution.py:21
  10.2 4.4 %collective-permute-start = (f32[1,3,512]{2,1,0:T(4,128)S(1)}, f32[1,3,512]{2,1,0:T(4,128)S(1)}, u32[]{:S(2)}, u32[]{:S(2)}) collective-permute-start(f32[1,3,512]{2,1,0:T(4,128)S(1)} %get-tuple-element.32), channel_id=1, source_target_pairs={{0,4},{4,0},{1,5},{5,1},{2,6},{6,2},{3,7},{7,3},{8,12},{12,8},{9,1... | collective-permute-start | bytes 18440 | tf_op jit(solution)/shard_map/ppermute | solution.py:19
  15.6 7.8 %collective-permute-start.3 = (f32[1,134,3]{2,1,0:T(8,128)S(1)}, f32[1,134,3]{2,1,0:T(8,128)S(1)}, u32[]{:S(2)}, u32[]{:S(2)}) collective-permute-start(f32[1,134,3]{2,1,0:T(8,128)S(1)} %get-tuple-element.29), channel_id=1, source_target_pairs={{1,0},{2,1},{3,2},{0,3},{5,4},{6,5},{7,6},{4,7},{9,8},{10,9},{11,1... | collective-permute-start | bytes 4832 | tf_op jit(solution)/shard_map/ppermute | solution.py:21
  19.7 6.1 %collective-permute-start.2 = (f32[1,134,3]{2,1,0:T(8,128)S(1)}, f32[1,134,3]{2,1,0:T(8,128)S(1)}, u32[]{:S(2)}, u32[]{:S(2)}) collective-permute-start(f32[1,134,3]{2,1,0:T(8,128)S(1)} %get-tuple-element.28), channel_id=1, source_target_pairs={{0,1},{1,2},{2,3},{3,0},{4,5},{5,6},{6,7},{7,4},{8,9},{9,10},{10,1... | collective-permute-start | bytes 4832 | tf_op jit(solution)/shard_map/ppermute | solution.py:19
  28.6 5.3 %collective-permute-start.5 = (f32[1,64,512]{2,1,0:T(8,128)S(1)}, f32[1,64,512]{2,1,0:T(8,128)S(1)}, u32[]{:S(2)}, u32[]{:S(2)}) collective-permute-start(f32[1,64,512]{2,1,0:T(8,128)S(1)} %get-tuple-element.31), channel_id=1, source_target_pairs={{4,0},{0,4},{5,1},{1,5},{6,2},{2,6},{7,3},{3,7},{12,8},{8,12},{13,... | collective-permute-start | bytes 393224 | tf_op jit(solution)/shard_map/ppermute | solution.py:21
  30.1 5.0 %collective-permute-start.4 = (f32[1,64,512]{2,1,0:T(8,128)S(1)}, f32[1,64,512]{2,1,0:T(8,128)S(1)}, u32[]{:S(2)}, u32[]{:S(2)}) collective-permute-start(f32[1,64,512]{2,1,0:T(8,128)S(1)} %get-tuple-element.30), channel_id=1, source_target_pairs={{0,4},{4,0},{1,5},{5,1},{2,6},{6,2},{3,7},{7,3},{8,12},{12,8},{9,1... | collective-permute-start | bytes 393224 | tf_op jit(solution)/shard_map/ppermute | solution.py:19
  35.1 0.6 copy-start.2
  36.5 82.4 %collective-permute-start.7 = (f32[1,256,64]{2,1,0:T(8,128)}, f32[1,256,64]{2,1,0:T(8,128)}, u32[]{:S(2)}, u32[]{:S(2)}) collective-permute-start(f32[1,256,64]{2,1,0:T(8,128)} %get-tuple-element.27), channel_id=1, source_target_pairs={{1,0},{2,1},{3,2},{0,3},{5,4},{6,5},{7,6},{4,7},{9,8},{10,9},{11,1... | collective-permute-start | bytes 196616 | tf_op jit(solution)/shard_map/ppermute | solution.py:21
  38.4 80.6 %collective-permute-start.6 = (f32[1,256,64]{2,1,0:T(8,128)}, f32[1,256,64]{2,1,0:T(8,128)}, u32[]{:S(2)}, u32[]{:S(2)}) collective-permute-start(f32[1,256,64]{2,1,0:T(8,128)} %get-tuple-element.26), channel_id=1, source_target_pairs={{0,1},{1,2},{2,3},{3,0},{4,5},{5,6},{6,7},{7,4},{8,9},{9,10},{10,1... | collective-permute-start | bytes 196616 | tf_op jit(solution)/shard_map/ppermute | solution.py:19
  106.7 12.2 %copy-start.3 = (f32[1,64,512]{2,1,0:T(8,128)S(1)}, f32[1,64,512]{2,1,0:T(8,128)}, u32[]{:S(2)}) copy-start(f32[1,64,512]{2,1,0:T(8,128)} %copy-done.2) | copy-start | bytes 393220
  106.7 13.5 %copy-start.4 = (s32[128,512]{1,0:T(8,128)S(1)}, s32[128,512]{1,0:T(8,128)}, u32[]{:S(2)}) copy-start(s32[128,512]{1,0:T(8,128)} %param.9) | copy-start | bytes 786436
  159.8 6.0 %copy-start.1 = (f32[16,8,64,8]{3,2,1,0:T(8,128)S(1)}, f32[16,8,64,8]{3,2,1,0:T(8,128)}, u32[]{:S(2)}) copy-start(f32[16,8,64,8]{3,2,1,0:T(8,128)} %mul.223) | copy-start | bytes 786436
  165.8 5.1 %copy-start = (f32[16,8,64,8]{3,2,1,0:T(8,128)S(1)}, f32[16,8,64,8]{3,2,1,0:T(8,128)}, u32[]{:S(2)}) copy-start(f32[16,8,64,8]{3,2,1,0:T(8,128)} %mul.227) | copy-start | bytes 786436
  165.8 10.1 %slice-start.6 = ((s8[8388608]{0:T(1024)(128)(4,1)}), s8[4194304]{0:T(1024)(128)(4,1)S(1)}, s32[]{:S(2)}) async-start(s8[8388608]{0:T(1024)(128)(4,1)} %bitcast.106), calls=%async_computation.7 | async-start | bytes 8388608
  170.9 5.1 %slice-start.7 = ((s8[8388608]{0:T(1024)(128)(4,1)}), s8[4194304]{0:T(1024)(128)(4,1)S(1)}, s32[]{:S(2)}) async-start(s8[8388608]{0:T(1024)(128)(4,1)} %bitcast.106), calls=%async_computation.8 | async-start | bytes 8388608
  170.9 8.9 %slice-start.4 = ((s8[8388608]{0:T(1024)(128)(4,1)}), s8[4194304]{0:T(1024)(128)(4,1)S(1)}, s32[]{:S(2)}) async-start(s8[8388608]{0:T(1024)(128)(4,1)} %bitcast.104), calls=%async_computation.5 | async-start | bytes 8388608
  176.0 3.8 %slice-start.5 = ((s8[8388608]{0:T(1024)(128)(4,1)}), s8[4194304]{0:T(1024)(128)(4,1)S(1)}, s32[]{:S(2)}) async-start(s8[8388608]{0:T(1024)(128)(4,1)} %bitcast.104), calls=%async_computation.6 | async-start | bytes 8388608
  179.8 9.8 %slice-start.2 = ((s8[8388608]{0:T(1024)(128)(4,1)}), s8[4194304]{0:T(1024)(128)(4,1)S(1)}, s32[]{:S(2)}) async-start(s8[8388608]{0:T(1024)(128)(4,1)} %bitcast.102), calls=%async_computation.3 | async-start | bytes 8388608
  183.6 6.0 %slice-start.3 = ((s8[8388608]{0:T(1024)(128)(4,1)}), s8[4194304]{0:T(1024)(128)(4,1)S(1)}, s32[]{:S(2)}) async-start(s8[8388608]{0:T(1024)(128)(4,1)} %bitcast.102), calls=%async_computation.4 | async-start | bytes 8388608
  183.6 9.9 %slice-start = ((s8[8388608]{0:T(1024)(128)(4,1)}), s8[4194304]{0:T(1024)(128)(4,1)S(1)}, s32[]{:S(2)}) async-start(s8[8388608]{0:T(1024)(128)(4,1)} %bitcast.100), calls=%async_computation.1 | async-start | bytes 8388608
  189.6 3.8 %slice-start.1 = ((s8[8388608]{0:T(1024)(128)(4,1)}), s8[4194304]{0:T(1024)(128)(4,1)S(1)}, s32[]{:S(2)}) async-start(s8[8388608]{0:T(1024)(128)(4,1)} %bitcast.100), calls=%async_computation.2 | async-start | bytes 8388608
  197.1 0.7 copy-start.5
Sparse Core Ops, SparseCore 0:
  197.9 32.0 all-reduce.1
where the time goes:
time: 239 us; the launch traced here: 238 us
  local copies, waits for them, and re-layouts  96.4 us (40%)
  other arithmetic  53.4 us (22%)
  between operations  41.5 us (17%)
  waiting for transfers between devices  35.9 us (15%)
  starting transfers between devices  11.2 us (5%)
    convert_element_type x9, local copies, waits for them, and re-layouts, on_device(): terms = weights[d].astype(jnp.float32) * masked[None]  57.9 us
    reduce_sum x9, other arithmetic, on_device(): terms.reshape(2, rows // SUB, SUB, cols // SUB, SUB).sum(axis=(2, 4))  42.9 us
    mul x9, local copies, waits for them, and re-layouts, on_device(): terms = weights[d].astype(jnp.float32) * masked[None]  32.8 us
    psum x1, waiting for transfers between devices, on_device(): return lax.psum(local_slopes, 'layer')  32.3 us
    ppermute x4, starting transfers between devices, padded(): lax.ppermute(head, axis, [((i + 1) % count, i) for i in range(count)])  10.5 us
  transfers between devices with their start and end apart: 9, of which 3 were waited for; matrix products, arithmetic and copies ran while one was open for 27% of the time, Pallas kernels for 0%

commit v1 on v0

--- a/solution.py
+++ b/solution.py
@@ -60,7 +60,7 @@
         terms = weights[d].astype(jnp.float32) * masked[None]
         results.append(terms.reshape(2, rows // SUB, SUB, cols // SUB, SUB).sum(axis=(2, 4)))
     local_slopes = jnp.stack(results, axis=1)
-    return lax.psum(local_slopes, "layer")
+    return jnp.sum(lax.all_gather(local_slopes, "layer"), axis=0)
 
 
 def solution(mesh):

time: 239 us -> 200 us (0.84)
  waiting for transfers between devices: 35.9 us -> 3.61 us
  between operations: 41.5 us -> 28.2 us
  blocking collectives: 0 us -> 7.54 us
    psum x1 -> x0, waiting for transfers between devices: 32.3 us -> none  [on_device(): return lax.psum(local_slopes, 'layer')]
    all_gather x0 -> x1, blocking collectives: none -> 7.54 us  [on_device(): return jnp.sum(lax.all_gather(local_slopes, 'layer'), axis=0)]
  transfers between devices with their start and end apart: 9 -> 8, of which waited for: 3 -> 2; matrix products, arithmetic and copies ran while one was open for 27% -> 32% of each run, Pallas kernels for 0% -> 0%
where the time goes in v1:
time: 200 us; the launch traced here: 199 us
  local copies, waits for them, and re-layouts  94.8 us (47%)
  other arithmetic  53.5 us (27%)
  between operations  28.2 us (14%)
  starting transfers between devices  11.2 us (6%)
  blocking collectives  7.54 us (4%)
  waiting for transfers between devices  3.61 us (2%)
    convert_element_type x9, local copies, waits for them, and re-layouts, on_device(): terms = weights[d].astype(jnp.float32) * masked[None]  57.8 us
    reduce_sum x9, other arithmetic, on_device(): terms.reshape(2, rows // SUB, SUB, cols // SUB, SUB).sum(axis=(2, 4))  42.9 us
    mul x9, local copies, waits for them, and re-layouts, on_device(): terms = weights[d].astype(jnp.float32) * masked[None]  32.9 us
    ppermute x4, starting transfers between devices, padded(): lax.ppermute(head, axis, [((i + 1) % count, i) for i in range(count)])  10.5 us
    all_gather x1, blocking collectives, on_device(): return jnp.sum(lax.all_gather(local_slopes, 'layer'), axis=0)  7.54 us
  transfers between devices with their start and end apart: 8, of which 2 were waited for; matrix products, arithmetic and copies ran while one was open for 32% of the time, Pallas kernels for 0%

profile of v1, /device:TPU:0, one launch (start us, length us, event | category | flops | bytes accessed | tf_op | source)
XLA Modules:
  0.0 198.9 jit_solution(3416383736022666705)
XLA Ops:
  0.8 2.9 %collective-permute-start.1 = (f32[1,3,512]{2,1,0:T(4,128)S(1)}, f32[1,3,512]{2,1,0:T(4,128)S(1)}, u32[]{:S(2)}, u32[]{:S(2)}) collective-permute-start(f32[1,3,512]{2,1,0:T(4,128)S(1)} %get-tuple-element.33), channel_id=1, source_target_pairs={{4,0},{0,4},{5,1},{1,5},{6,2},{2,6},{7,3},{3,7},{12,8},{8,12},{13,... | collective-permute-start | bytes 18440 | tf_op jit(solution)/shard_map/ppermute | solution.py:21
  9.1 4.1 %collective-permute-start.3 = (f32[1,134,3]{2,1,0:T(8,128)S(1)}, f32[1,134,3]{2,1,0:T(8,128)S(1)}, u32[]{:S(2)}, u32[]{:S(2)}) collective-permute-start(f32[1,134,3]{2,1,0:T(8,128)S(1)} %get-tuple-element.29), channel_id=1, source_target_pairs={{1,0},{2,1},{3,2},{0,3},{5,4},{6,5},{7,6},{4,7},{9,8},{10,9},{11,1... | collective-permute-start | bytes 4832 | tf_op jit(solution)/shard_map/ppermute | solution.py:21
  16.9 2.4 %collective-permute-done.2 = f32[1,134,3]{2,1,0:T(8,128)S(1)} collective-permute-done((f32[1,134,3]{2,1,0:T(8,128)S(1)}, f32[1,134,3]{2,1,0:T(8,128)S(1)}, u32[]{:S(2)}, u32[]{:S(2)}) %collective-permute-start.2) | collective-permute-done | bytes 1640 | tf_op jit(solution)/shard_map/ppermute | solution.py:19
  24.2 3.2 %slice_convert_fusion = (f32[1,2,128,512]{3,2,1,0:T(8,128)S(1)}, f32[1,2,128,512]{3,2,1,0:T(8,128)S(1)}, f32[1,2,128,512]{3,2,1,0:T(8,128)S(1)}, f32[1,2,128,512...) fusion(bf16[9,2,128,512]{3,2,1,0:T(8,128)(2,1)} %param.8), kind=kLoop, calls=%fused_computation.20 | loop fusion | flops 1179648 | bytes 7077888 | tf_op jit(solution)/shard_map/convert_element_type | solution.py:60
  54.6 7.1 %reshape.200 = f32[2,16,8,64,8]{4,3,2,1,0:T(8,128)} reshape(f32[1,2,128,512]{3,2,1,0:T(8,128)} %get-tuple-element.16) | data formatting | bytes 1048576 | tf_op jit(solution)/shard_map/convert_element_type | solution.py:60
  61.7 7.0 %reshape.201 = f32[2,16,8,64,8]{4,3,2,1,0:T(8,128)} reshape(f32[1,2,128,512]{3,2,1,0:T(8,128)} %get-tuple-element.15) | data formatting | bytes 1048576 | tf_op jit(solution)/shard_map/convert_element_type | solution.py:60
  68.7 7.0 %reshape.202 = f32[2,16,8,64,8]{4,3,2,1,0:T(8,128)} reshape(f32[1,2,128,512]{3,2,1,0:T(8,128)} %get-tuple-element.14) | data formatting | bytes 1048576 | tf_op jit(solution)/shard_map/convert_element_type | solution.py:60
  75.8 6.1 %reshape.203 = f32[2,16,8,64,8]{4,3,2,1,0:T(8,128)} reshape(f32[1,2,128,512]{3,2,1,0:T(8,128)S(1)} %get-tuple-element.13) | data formatting | bytes 1048576 | tf_op jit(solution)/shard_map/convert_element_type | solution.py:60
  81.9 6.1 %reshape.204 = f32[2,16,8,64,8]{4,3,2,1,0:T(8,128)} reshape(f32[1,2,128,512]{3,2,1,0:T(8,128)S(1)} %get-tuple-element.12) | data formatting | bytes 1048576 | tf_op jit(solution)/shard_map/convert_element_type | solution.py:60
  88.0 6.1 %reshape.205 = f32[2,16,8,64,8]{4,3,2,1,0:T(8,128)} reshape(f32[1,2,128,512]{3,2,1,0:T(8,128)S(1)} %get-tuple-element.11) | data formatting | bytes 1048576 | tf_op jit(solution)/shard_map/convert_element_type | solution.py:60
  94.1 6.1 %reshape.206 = f32[2,16,8,64,8]{4,3,2,1,0:T(8,128)} reshape(f32[1,2,128,512]{3,2,1,0:T(8,128)S(1)} %get-tuple-element.10) | data formatting | bytes 1048576 | tf_op jit(solution)/shard_map/convert_element_type | solution.py:60
  100.2 6.1 %reshape.207 = f32[2,16,8,64,8]{4,3,2,1,0:T(8,128)} reshape(f32[1,2,128,512]{3,2,1,0:T(8,128)S(1)} %get-tuple-element.17) | data formatting | bytes 1048576 | tf_op jit(solution)/shard_map/convert_element_type | solution.py:60
  106.3 6.1 %reshape.208 = f32[2,16,8,64,8]{4,3,2,1,0:T(8,128)} reshape(f32[1,2,128,512]{3,2,1,0:T(8,128)S(1)} %get-tuple-element.9) | data formatting | bytes 1048576 | tf_op jit(solution)/shard_map/convert_element_type | solution.py:60
  114.6 3.7 %mul.215 = f32[16,8,64,8]{3,2,1,0:T(8,128)} reshape(f32[128,512]{1,0:T(8,128)S(1)} %get-tuple-element.25) | data formatting | bytes 524288 | tf_op jit(solution)/shard_map/mul | solution.py:60
  118.3 5.9 %multiply_reduce_fusion.8 = f32[2,16,64]{2,1,0:T(8,128)S(1)} fusion(f32[2,16,8,64,8]{4,3,2,1,0:T(8,128)} %reshape.200, f32[16,8,64,8]{3,2,1,0:T(8,128)} %mul.215), kind=kLoop, calls=%fused_computation.8 | loop fusion | flops 260096 | bytes 794624 | tf_op jit(solution)/shard_map/reduce_sum | solution.py:61
  124.2 3.7 %mul.219 = f32[16,8,64,8]{3,2,1,0:T(8,128)} reshape(f32[128,512]{1,0:T(8,128)S(1)} %get-tuple-element.24) | data formatting | bytes 524288 | tf_op jit(solution)/shard_map/mul | solution.py:60
  127.9 3.6 %mul.223 = f32[16,8,64,8]{3,2,1,0:T(8,128)} reshape(f32[128,512]{1,0:T(8,128)S(1)} %get-tuple-element.23) | data formatting | bytes 524288 | tf_op jit(solution)/shard_map/mul | solution.py:60
  131.5 3.6 %mul.227 = f32[16,8,64,8]{3,2,1,0:T(8,128)} reshape(f32[128,512]{1,0:T(8,128)S(1)} %get-tuple-element.22) | data formatting | bytes 524288 | tf_op jit(solution)/shard_map/mul | solution.py:60
  135.1 3.7 %mul.231 = f32[16,8,64,8]{3,2,1,0:T(8,128)} reshape(f32[128,512]{1,0:T(8,128)S(1)} %get-tuple-element.21) | data formatting | bytes 524288 | tf_op jit(solution)/shard_map/mul | solution.py:60
  138.8 3.6 %mul.235 = f32[16,8,64,8]{3,2,1,0:T(8,128)} reshape(f32[128,512]{1,0:T(8,128)S(1)} %get-tuple-element.20) | data formatting | bytes 524288 | tf_op jit(solution)/shard_map/mul | solution.py:60
  142.4 3.7 %mul.239 = f32[16,8,64,8]{3,2,1,0:T(8,128)} reshape(f32[128,512]{1,0:T(8,128)S(1)} %get-tuple-element.19) | data formatting | bytes 524288 | tf_op jit(solution)/shard_map/mul | solution.py:60
  146.1 3.6 %mul.243 = f32[16,8,64,8]{3,2,1,0:T(8,128)} reshape(f32[128,512]{1,0:T(8,128)S(1)} %get-tuple-element.18) | data formatting | bytes 524288 | tf_op jit(solution)/shard_map/mul | solution.py:60
  149.7 3.7 %mul.247 = f32[16,8,64,8]{3,2,1,0:T(8,128)} reshape(f32[128,512]{1,0:T(8,128)S(1)} %get-tuple-element.5) | data formatting | bytes 524288 | tf_op jit(solution)/shard_map/mul | solution.py:60
  153.4 6.0 %multiply_reduce_fusion.7 = f32[2,16,64]{2,1,0:T(8,128)S(1)} fusion(f32[2,16,8,64,8]{4,3,2,1,0:T(8,128)} %reshape.201, f32[16,8,64,8]{3,2,1,0:T(8,128)} %mul.219), kind=kLoop, calls=%fused_computation.7 | loop fusion | flops 260096 | bytes 794624 | tf_op jit(solution)/shard_map/reduce_sum | solution.py:61
  159.4 5.0 %multiply_reduce_fusion.6 = f32[2,16,64]{2,1,0:T(8,128)S(1)} fusion(f32[2,16,8,64,8]{4,3,2,1,0:T(8,128)} %reshape.202, f32[16,8,64,8]{3,2,1,0:T(8,128)S(1)} %copy-done.1), kind=kLoop, calls=%fused_computation.6 | loop fusion | flops 260096 | bytes 794624 | tf_op jit(solution)/shard_map/reduce_sum | solution.py:61
  164.5 5.0 %multiply_reduce_fusion.5 = f32[2,16,64]{2,1,0:T(8,128)S(1)} fusion(f32[2,16,8,64,8]{4,3,2,1,0:T(8,128)} %reshape.203, f32[16,8,64,8]{3,2,1,0:T(8,128)S(1)} %copy-done), kind=kLoop, calls=%fused_computation.5 | loop fusion | flops 260096 | bytes 794624 | tf_op jit(solution)/shard_map/reduce_sum | solution.py:61
  169.6 3.8 %multiply_reduce_fusion.4 = f32[2,16,64]{2,1,0:T(8,128)S(1)} fusion(f32[2,16,8,64,8]{4,3,2,1,0:T(8,128)S(1)} %bitcast.108, f32[16,8,64,8]{3,2,1,0:T(8,128)} %mul.231), kind=kLoop, calls=%fused_computation.4 | loop fusion | flops 260096 | bytes 794624 | tf_op jit(solution)/shard_map/reduce_sum | solution.py:61
  173.4 3.8 %multiply_reduce_fusion.3 = f32[2,16,64]{2,1,0:T(8,128)S(1)} fusion(f32[2,16,8,64,8]{4,3,2,1,0:T(8,128)S(1)} %bitcast.106, f32[16,8,64,8]{3,2,1,0:T(8,128)} %mul.235), kind=kLoop, calls=%fused_computation.3 | loop fusion | flops 260096 | bytes 794624 | tf_op jit(solution)/shard_map/reduce_sum | solution.py:61
  177.2 6.0 %multiply_reduce_fusion.2 = f32[2,16,64]{2,1,0:T(8,128)S(1)} fusion(f32[2,16,8,64,8]{4,3,2,1,0:T(8,128)} %reshape.206, f32[16,8,64,8]{3,2,1,0:T(8,128)} %mul.239), kind=kLoop, calls=%fused_computation.2 | loop fusion | flops 260096 | bytes 794624 | tf_op jit(solution)/shard_map/reduce_sum | solution.py:61
  183.2 3.8 %multiply_reduce_fusion.1 = f32[2,16,64]{2,1,0:T(8,128)S(1)} fusion(f32[2,16,8,64,8]{4,3,2,1,0:T(8,128)S(1)} %bitcast.104, f32[16,8,64,8]{3,2,1,0:T(8,128)} %mul.243), kind=kLoop, calls=%fused_computation.1 | loop fusion | flops 260096 | bytes 794624 | tf_op jit(solution)/shard_map/reduce_sum | solution.py:61
  187.0 3.6 %multiply_reduce_fusion = f32[2,16,64]{2,1,0:T(8,128)S(1)} fusion(f32[2,16,8,64,8]{4,3,2,1,0:T(8,128)S(1)} %bitcast.102, f32[16,8,64,8]{3,2,1,0:T(8,128)} %mul.247), kind=kLoop, calls=%fused_computation | loop fusion | flops 260096 | bytes 794624 | tf_op jit(solution)/shard_map/reduce_sum | solution.py:61
  190.6 7.5 %all-gather = f32[8,9,16,64]{3,2,0,1:T(8,128)S(1)} all-gather(f32[2,9,16,64]{3,2,0,1:T(8,128)S(1)} %constant_dynamic-update-slice_fusion), channel_id=2, replica_groups=mesh['layer'=4,'tx'=2,'ty'=4] {'layer'}, dimensions={0}, use_global_device_ids=true | all-gather | bytes 368640 | tf_op jit(solution)/shard_map/all_gather | solution.py:63
  (69 shorter events, 16.8 us)
Async XLA Ops:
  0.0 32.0 %copy-start.5 = (s32[1,9,2]{1,2,0:T(2,128)S(1)}, s32[1,9,2]{1,2,0:T(2,128)}, u32[]{:S(2)}) copy-start(s32[1,9,2]{1,2,0:T(2,128)} %param.7) | copy-start | bytes 220
  0.8 7.3 %collective-permute-start.1 = (f32[1,3,512]{2,1,0:T(4,128)S(1)}, f32[1,3,512]{2,1,0:T(4,128)S(1)}, u32[]{:S(2)}, u32[]{:S(2)}) collective-permute-start(f32[1,3,512]{2,1,0:T(4,128)S(1)} %get-tuple-element.33), channel_id=1, source_target_pairs={{4,0},{0,4},{5,1},{1,5},{6,2},{2,6},{7,3},{3,7},{12,8},{8,12},{13,... | collective-permute-start | bytes 18440 | tf_op jit(solution)/shard_map/ppermute | solution.py:21
  3.7 4.4 %collective-permute-start = (f32[1,3,512]{2,1,0:T(4,128)S(1)}, f32[1,3,512]{2,1,0:T(4,128)S(1)}, u32[]{:S(2)}, u32[]{:S(2)}) collective-permute-start(f32[1,3,512]{2,1,0:T(4,128)S(1)} %get-tuple-element.32), channel_id=1, source_target_pairs={{0,4},{4,0},{1,5},{5,1},{2,6},{6,2},{3,7},{7,3},{8,12},{12,8},{9,1... | collective-permute-start | bytes 18440 | tf_op jit(solution)/shard_map/ppermute | solution.py:19
  9.1 7.8 %collective-permute-start.3 = (f32[1,134,3]{2,1,0:T(8,128)S(1)}, f32[1,134,3]{2,1,0:T(8,128)S(1)}, u32[]{:S(2)}, u32[]{:S(2)}) collective-permute-start(f32[1,134,3]{2,1,0:T(8,128)S(1)} %get-tuple-element.29), channel_id=1, source_target_pairs={{1,0},{2,1},{3,2},{0,3},{5,4},{6,5},{7,6},{4,7},{9,8},{10,9},{11,1... | collective-permute-start | bytes 4832 | tf_op jit(solution)/shard_map/ppermute | solution.py:21
  13.2 6.1 %collective-permute-start.2 = (f32[1,134,3]{2,1,0:T(8,128)S(1)}, f32[1,134,3]{2,1,0:T(8,128)S(1)}, u32[]{:S(2)}, u32[]{:S(2)}) collective-permute-start(f32[1,134,3]{2,1,0:T(8,128)S(1)} %get-tuple-element.28), channel_id=1, source_target_pairs={{0,1},{1,2},{2,3},{3,0},{4,5},{5,6},{6,7},{7,4},{8,9},{9,10},{10,1... | collective-permute-start | bytes 4832 | tf_op jit(solution)/shard_map/ppermute | solution.py:19
  22.1 5.3 %collective-permute-start.5 = (f32[1,64,512]{2,1,0:T(8,128)S(1)}, f32[1,64,512]{2,1,0:T(8,128)S(1)}, u32[]{:S(2)}, u32[]{:S(2)}) collective-permute-start(f32[1,64,512]{2,1,0:T(8,128)S(1)} %get-tuple-element.31), channel_id=1, source_target_pairs={{4,0},{0,4},{5,1},{1,5},{6,2},{2,6},{7,3},{3,7},{12,8},{8,12},{13,... | collective-permute-start | bytes 393224 | tf_op jit(solution)/shard_map/ppermute | solution.py:21
  23.6 5.0 %collective-permute-start.4 = (f32[1,64,512]{2,1,0:T(8,128)S(1)}, f32[1,64,512]{2,1,0:T(8,128)S(1)}, u32[]{:S(2)}, u32[]{:S(2)}) collective-permute-start(f32[1,64,512]{2,1,0:T(8,128)S(1)} %get-tuple-element.30), channel_id=1, source_target_pairs={{0,4},{4,0},{1,5},{5,1},{2,6},{6,2},{3,7},{7,3},{8,12},{12,8},{9,1... | collective-permute-start | bytes 393224 | tf_op jit(solution)/shard_map/ppermute | solution.py:19
  28.6 0.7 copy-start.2
  30.0 82.5 %collective-permute-start.7 = (f32[1,256,64]{2,1,0:T(8,128)}, f32[1,256,64]{2,1,0:T(8,128)}, u32[]{:S(2)}, u32[]{:S(2)}) collective-permute-start(f32[1,256,64]{2,1,0:T(8,128)} %get-tuple-element.27), channel_id=1, source_target_pairs={{1,0},{2,1},{3,2},{0,3},{5,4},{6,5},{7,6},{4,7},{9,8},{10,9},{11,1... | collective-permute-start | bytes 196616 | tf_op jit(solution)/shard_map/ppermute | solution.py:21
  31.9 80.5 %collective-permute-start.6 = (f32[1,256,64]{2,1,0:T(8,128)}, f32[1,256,64]{2,1,0:T(8,128)}, u32[]{:S(2)}, u32[]{:S(2)}) collective-permute-start(f32[1,256,64]{2,1,0:T(8,128)} %get-tuple-element.26), channel_id=1, source_target_pairs={{0,1},{1,2},{2,3},{3,0},{4,5},{5,6},{6,7},{7,4},{8,9},{9,10},{10,1... | collective-permute-start | bytes 196616 | tf_op jit(solution)/shard_map/ppermute | solution.py:19
  100.2 12.2 %copy-start.3 = (f32[1,64,512]{2,1,0:T(8,128)S(1)}, f32[1,64,512]{2,1,0:T(8,128)}, u32[]{:S(2)}) copy-start(f32[1,64,512]{2,1,0:T(8,128)} %copy-done.2) | copy-start | bytes 393220
  100.2 13.5 %copy-start.4 = (s32[128,512]{1,0:T(8,128)S(1)}, s32[128,512]{1,0:T(8,128)}, u32[]{:S(2)}) copy-start(s32[128,512]{1,0:T(8,128)} %param.9) | copy-start | bytes 786436
  153.4 6.0 %copy-start.1 = (f32[16,8,64,8]{3,2,1,0:T(8,128)S(1)}, f32[16,8,64,8]{3,2,1,0:T(8,128)}, u32[]{:S(2)}) copy-start(f32[16,8,64,8]{3,2,1,0:T(8,128)} %mul.223) | copy-start | bytes 786436
  159.4 5.1 %copy-start = (f32[16,8,64,8]{3,2,1,0:T(8,128)S(1)}, f32[16,8,64,8]{3,2,1,0:T(8,128)}, u32[]{:S(2)}) copy-start(f32[16,8,64,8]{3,2,1,0:T(8,128)} %mul.227) | copy-start | bytes 786436
  159.4 10.1 %slice-start.6 = ((s8[8388608]{0:T(1024)(128)(4,1)}), s8[4194304]{0:T(1024)(128)(4,1)S(1)}, s32[]{:S(2)}) async-start(s8[8388608]{0:T(1024)(128)(4,1)} %bitcast.107), calls=%async_computation.6 | async-start | bytes 8388608
  164.5 5.1 %slice-start.7 = ((s8[8388608]{0:T(1024)(128)(4,1)}), s8[4194304]{0:T(1024)(128)(4,1)S(1)}, s32[]{:S(2)}) async-start(s8[8388608]{0:T(1024)(128)(4,1)} %bitcast.107), calls=%async_computation.7 | async-start | bytes 8388608
  164.5 8.9 %slice-start.4 = ((s8[8388608]{0:T(1024)(128)(4,1)}), s8[4194304]{0:T(1024)(128)(4,1)S(1)}, s32[]{:S(2)}) async-start(s8[8388608]{0:T(1024)(128)(4,1)} %bitcast.105), calls=%async_computation.4 | async-start | bytes 8388608
  169.5 3.8 %slice-start.5 = ((s8[8388608]{0:T(1024)(128)(4,1)}), s8[4194304]{0:T(1024)(128)(4,1)S(1)}, s32[]{:S(2)}) async-start(s8[8388608]{0:T(1024)(128)(4,1)} %bitcast.105), calls=%async_computation.5 | async-start | bytes 8388608
  173.4 9.8 %slice-start.2 = ((s8[8388608]{0:T(1024)(128)(4,1)}), s8[4194304]{0:T(1024)(128)(4,1)S(1)}, s32[]{:S(2)}) async-start(s8[8388608]{0:T(1024)(128)(4,1)} %bitcast.103), calls=%async_computation.2 | async-start | bytes 8388608
  177.1 6.1 %slice-start.3 = ((s8[8388608]{0:T(1024)(128)(4,1)}), s8[4194304]{0:T(1024)(128)(4,1)S(1)}, s32[]{:S(2)}) async-start(s8[8388608]{0:T(1024)(128)(4,1)} %bitcast.103), calls=%async_computation.3 | async-start | bytes 8388608
  177.1 9.9 %slice-start = ((s8[8388608]{0:T(1024)(128)(4,1)}), s8[4194304]{0:T(1024)(128)(4,1)S(1)}, s32[]{:S(2)}) async-start(s8[8388608]{0:T(1024)(128)(4,1)} %bitcast.101), calls=%async_computation | async-start | bytes 8388608
  183.2 3.8 %slice-start.1 = ((s8[8388608]{0:T(1024)(128)(4,1)}), s8[4194304]{0:T(1024)(128)(4,1)S(1)}, s32[]{:S(2)}) async-start(s8[8388608]{0:T(1024)(128)(4,1)} %bitcast.101), calls=%async_computation.1 | async-start | bytes 8388608
